TPU v7x, 32 devices: a whole 2x2x4 slice. The times are simulated.
32 devices in a mesh: sx: 4 (over x, core), sy: 4 (over z), ch: 2 (over y).
Axes of the slice: x: 2, y: 2, z: 4, core: 2. Of those that a mesh axis runs over, the one named last changes fastest.
Arguments:
- volume: bfloat16 [512, 32, 512], P('ch', 'sx', 'sy'), may hold values from -6 to 6
- weight: bfloat16 [3, 3, 3, 512, 512], P(None, None, None, 'ch'), may hold values from -0.0546875 to 0.0546875
- bias: float32 [512], P('ch'), may hold values from -3 to 3
Outputs:
- convolved: bfloat16 [512, 32, 512], P('ch', 'sx', 'sy')
All inputs are finite; a program needn't handle non-finite values.
Results may differ from a plain program's by a relative error of at most 0.001.
Values may be sent and summed in bfloat16 or wider, within the bound.
No kernel may reach another device: no remote copies, remote signals or barrier semaphores. Data moves between devices by JAX's collectives and lax.ppermute only.
A program may use at most 192 MiB of HBM per device.

v0:
```python
import jax
import jax.numpy as jnp
from jax import lax
from jax.sharding import PartitionSpec as P

CZ = 16


def padded(cells, sides, width):
    for axis, dim in sides:
        count = lax.axis_size(axis)
        ends = count - 1
        head = lax.slice_in_dim(cells, 0, width, axis=dim)
        tail = lax.slice_in_dim(cells, cells.shape[dim] - width, cells.shape[dim], axis=dim)
        cells = jnp.concatenate(
            [
                lax.ppermute(tail, axis, [(i, (i + 1) % count) for i in range(ends)]),
                cells,
                lax.ppermute(head, axis, [((i + 1) % count, i) for i in range(ends)]),
            ],
            axis=dim,
        )
    return cells


def add_taps(running, extended, filters, cells_x, cells_y, cells_z):
    channels = extended.shape[0]
    outputs = running.shape[0]
    count = cells_x * cells_y * cells_z
    for along_x in range(3):
        for along_y in range(3):
            window = extended[:, along_x : along_x + cells_x, along_y : along_y + cells_y, :]
            window = window.reshape(channels, count)
            for along_z in range(3):
                tap_matrix = filters[along_x, along_y, along_z]
                product = jnp.dot(tap_matrix, window, preferred_element_type=jnp.float32)
                product = product.reshape(outputs, cells_x, cells_y, cells_z)
                if along_z == 0:
                    edge = jnp.zeros_like(product[..., :1])
                    product = jnp.concatenate([edge, product[..., :-1]], axis=3)
                elif along_z == 2:
                    edge = jnp.zeros_like(product[..., :1])
                    product = jnp.concatenate([product[..., 1:], edge], axis=3)
                running = running + product
    return running


def per_device(volume, weight, bias):
    local_in, cells_x, merged = volume.shape
    cells_z = CZ
    cells_y = merged // cells_z
    local_out = weight.shape[3]
    blocked = volume.reshape(local_in, cells_x, cells_y, cells_z)
    starting = jnp.zeros((local_out, cells_x, cells_y, cells_z), jnp.float32)
    gathered = lax.all_gather(blocked, "ch", axis=0, tiled=True)
    extended = padded(gathered, (("sx", 1), ("sy", 2)), 1)
    summed = add_taps(starting, extended, weight, cells_x, cells_y, cells_z)
    result = (summed + bias[:, None, None, None]).reshape(local_out, cells_x, cells_y * cells_z)
    return result.astype(jnp.bfloat16)


def solution(mesh):
    return jax.shard_map(
        per_device,
        mesh=mesh,
        in_specs=(P("ch", "sx", "sy"), P(None, None, None, "ch", None), P("ch")),
        out_specs=P("ch", "sx", "sy"),
        check_vma=False,
    )
```

profile of v0, /device:TPU:0, one launch (start us, length us, event | category | flops | bytes accessed | tf_op | source)
XLA Modules:
  0.0 82.0 jit_solution(11921416047235489947)
XLA Ops:
  6.5 0.0 all-gather.2.cloned.1.call-start
  6.5 2.1 %copy.6 = bf16[256,8,128]{0,2,1:T(8,128)(2,1)} copy(bf16[256,8,128]{2,1,0:T(8,128)(2,1)} %param.3) | data formatting | bytes 1048576 | tf_op args[0]
  8.7 0.0 all-gather.2.cloned.1.call-update
  8.7 24.2 %all-gather.2.cloned.1.call-done = bf16[512,8,8,16]{0,3,2,1:T(8,128)(2,1)} async-done(((bf16[256,8,8,16]{0,3,2,1:T(8,128)(2,1)}), bf16[512,8,8,16]{0,3,2,1:T(8,128)(2,1)}) %all-gather.2.cloned.1.call-update) | async-done | bytes 1048592 | tf_op jit(solution)/shard_map/all_gather | solution.py:55
  32.9 0.0 copy-start.1
  32.9 1.1 %fusion.90 = (bf16[512,1,8,16]{0,3,2,1:T(8,128)(2,1)S(1)}, bf16[512,1,8,16]{0,3,2,1:T(8,128)(2,1)S(1)}) fusion(bf16[512,8,8,16]{0,3,2,1:T(8,128)(2,1)} %all-gather.2.cloned.1.call-done), kind=kLoop, calls=%fused_computation.107 | loop fusion | bytes 524288 | tf_op jit(solution)/shard_map/slice | solution.py:13
  34.0 2.0 %collective-permute-start = (bf16[512,1,8,16]{0,3,2,1:T(8,128)(2,1)S(1)}, bf16[512,1,8,16]{0,3,2,1:T(8,128)(2,1)S(1)}, u32[]{:S(2)}, u32[]{:S(2)}) collective-permute-start(bf16[512,1,8,16]{0,3,2,1:T(8,128)(2,1)S(1)} %get-tuple-element.20), channel_id=1, source_target_pairs={{0,8},{8,16},{16,24},{1,9},{9,17},{17,25},{2,10},{10,18},{18,26},{... | collective-permute-start | bytes 393224 | tf_op jit(solution)/shard_map/ppermute | solution.py:17
  36.1 1.3 %collective-permute-start.1 = (bf16[512,1,8,16]{0,3,2,1:T(8,128)(2,1)S(1)}, bf16[512,1,8,16]{0,3,2,1:T(8,128)(2,1)S(1)}, u32[]{:S(2)}, u32[]{:S(2)}) collective-permute-start(bf16[512,1,8,16]{0,3,2,1:T(8,128)(2,1)S(1)} %get-tuple-element.19), channel_id=1, source_target_pairs={{8,0},{16,8},{24,16},{9,1},{17,9},{25,17},{10,2},{18,10},{26,18},{... | collective-permute-start | bytes 393224 | tf_op jit(solution)/shard_map/ppermute | solution.py:19
  37.4 2.8 %fusion.6 = f32[256,8,8,15]{0,3,2,1:T(8,128)} fusion(bf16[8,8,16,512]{3,2,1,0:T(8,128)(2,1)} %bitcast.238, bf16[3,3,3,256,512]{4,3,2,1,0:T(8,128)(2,1)} %param.4), kind=kOutput, calls=%fused_computation.18 | convolution fusion | flops 251658240 | bytes 2293760 | tf_op jit(solution)/shard_map/dot_general | solution.py:36
  40.1 1.8 %fusion.8 = f32[256,8,8,15]{0,3,2,1:T(8,128)S(1)} fusion(bf16[8,8,16,512]{3,2,1,0:T(8,128)(2,1)} %bitcast.239, bf16[3,3,3,256,512]{4,3,2,1,0:T(8,128)(2,1)} %param.4), kind=kOutput, calls=%fused_computation.20 | convolution fusion | flops 251658240 | bytes 2293760 | tf_op jit(solution)/shard_map/dot_general | solution.py:36
  41.9 0.0 collective-permute-done
  41.9 0.0 collective-permute-done.1
  41.9 2.2 %pad_maximum_fusion.3 = (bf16[512,8,8,16]{0,3,2,1:T(8,128)(2,1)S(1)}, bf16[512,8,8,16]{0,3,2,1:T(8,128)(2,1)S(1)}, bf16[512,10,8,16]{0,3,2,1:T(8,128)(2,1)S(1)}) fusion(bf16[512,8,8,16]{0,3,2,1:T(8,128)(2,1)} %all-gather.2.cloned.1.call-done, bf16[512,1,8,16]{0,3,2,1:T(8,128)(2,1)S(1)} %collective-permute-done, ...), kind=kLoop, calls=%fused_computation.22 | loop fusion | flops 4194304 | bytes 4456448 | tf_op jit(solution)/shard_map/concatenate | solution.py:15
  44.2 0.0 copy-done.1
  44.2 0.5 fusion.49
  44.7 0.5 fusion.51
  45.1 0.5 fusion.53
  45.6 0.5 fusion.19
  46.1 0.5 fusion.23
  46.6 3.4 %collective-permute-start.2 = (bf16[512,10,1,16]{0,3,2,1:T(8,128)(2,1)S(1)}, bf16[512,10,1,16]{0,3,2,1:T(8,128)(2,1)S(1)}, u32[]{:S(2)}, u32[]{:S(2)}) collective-permute-start(bf16[512,10,1,16]{0,3,2,1:T(8,128)(2,1)S(1)} %get-tuple-element.14), channel_id=1, source_target_pairs={{0,2},{2,4},{4,6},{1,3},{3,5},{5,7},{8,10},{10,12},{12,14},{9,11},... | collective-permute-start | bytes 491528 | tf_op jit(solution)/shard_map/ppermute | solution.py:17
  50.0 1.5 %collective-permute-start.3 = (bf16[512,10,1,16]{0,3,2,1:T(8,128)(2,1)S(1)}, bf16[512,10,1,16]{0,3,2,1:T(8,128)(2,1)S(1)}, u32[]{:S(2)}, u32[]{:S(2)}) collective-permute-start(bf16[512,10,1,16]{0,3,2,1:T(8,128)(2,1)S(1)} %get-tuple-element.15), channel_id=1, source_target_pairs={{2,0},{4,2},{6,4},{3,1},{5,3},{7,5},{10,8},{12,10},{14,12},{11,9},... | collective-permute-start | bytes 491528 | tf_op jit(solution)/shard_map/ppermute | solution.py:19
  51.5 0.1 slice.246
  51.6 0.1 slice.265
  51.7 0.5 fusion.21
  52.2 0.9 %collective-permute-done.2 = bf16[512,10,1,16]{0,3,2,1:T(8,128)(2,1)S(1)} collective-permute-done((bf16[512,10,1,16]{0,3,2,1:T(8,128)(2,1)S(1)}, bf16[512,10,1,16]{0,3,2,1:T(8,128)(2,1)S(1)}, u32[]{:S(2)}, u32[]{:S(2)}) %collective-permute-start.2) | collective-permute-done | bytes 163872 | tf_op jit(solution)/shard_map/ppermute | solution.py:17
  53.1 4.7 %collective-permute-done.3 = bf16[512,10,1,16]{0,3,2,1:T(8,128)(2,1)S(1)} collective-permute-done((bf16[512,10,1,16]{0,3,2,1:T(8,128)(2,1)S(1)}, bf16[512,10,1,16]{0,3,2,1:T(8,128)(2,1)S(1)}, u32[]{:S(2)}, u32[]{:S(2)}) %collective-permute-start.3) | collective-permute-done | bytes 163872 | tf_op jit(solution)/shard_map/ppermute | solution.py:19
  57.8 0.6 fusion.5
  58.4 0.5 fusion.37
  58.9 0.5 fusion.41
  59.3 0.5 fusion.43
  59.8 0.5 fusion.47
  60.3 0.5 fusion.55
  60.7 0.5 fusion.59
  61.2 0.5 fusion.45
  61.7 0.5 fusion.39
  62.1 0.5 fusion.57
  62.6 0.5 fusion.35
  63.1 0.5 fusion.31
  63.5 0.5 fusion.13
  64.0 0.5 fusion.17
  64.5 0.5 fusion.25
  64.9 0.5 fusion.29
  65.4 0.5 fusion.33
  65.9 0.5 fusion.27
  66.3 0.0 copy-start
  66.4 0.5 fusion.15
  66.8 0.1 slice.244
  66.9 0.1 slice.251
  67.1 0.1 slice.255
  67.2 0.1 slice.261
  67.4 0.1 slice.263
  67.5 1.1 %slice.267 = f32[256,8,8,15]{0,3,2,1:T(8,128)} slice(f32[256,8,8,16]{0,3,2,1:T(8,128)S(1)} %bitcast.253), slice={[0:256], [0:8], [0:8], [1:16]} | slice | bytes 1966080 | tf_op jit(solution)/shard_map/slice | solution.py:43
  68.6 0.0 copy-done
  68.6 0.0 copy-start.2
  68.6 2.6 %fusion.1 = f32[256,8,8,16]{0,3,2,1:T(8,128)S(1)} fusion(f32[256,8,8,15]{0,3,2,1:T(8,128)S(1)} %bitcast.248, f32[256,8,8,15]{0,3,2,1:T(8,128)} %fusion.6, f32[256,8,8,15]{0,3,2,1:T(8,128)S(1)} %fusion.8, f32[256,8,8,15]{0,3,2,1:T(8,128)S(1)} %slice.255, f32[256,8,8,16]{0,3,2,1:T(8,128)S(1)} %bitcast.246, f32[256,8,8,15]{0,3,2,1:T(8,128)S(1)} %bitcast.242, ...), kind=kOutput, calls=%fused_computation.10 | convolution fusion | flops 272367616 | bytes 18022400 | tf_op jit(solution)/shard_map/dot_general | solution.py:36
  71.2 0.0 copy-done.2
  71.3 2.9 %add_convert_fusion = bf16[256,8,8,16]{0,3,2,1:T(8,128)(2,1)S(1)} fusion(f32[256,8,8,15]{0,3,2,1:T(8,128)} %slice.267, f32[256,8,8,16]{0,3,2,1:T(8,128)S(1)} %bitcast.263, f32[256,8,8,15]{0,3,2,1:T(8,128)S(1)} %bitcast.259, f32[256,8,8,15]{0,3,2,1:T(8,128)S(1)} %slice.265, f32[256,8,8,16]{0,3,2,1:T(8,128)S(1)} %bitcast.258, ...), kind=kLoop, calls=%fused_computation.23 | loop fusion | flops 3407872 | bytes 12649472 | tf_op jit(solution)/shard_map/convert_element_type | solution.py:59
  74.1 1.1 %copy.7 = bf16[256,8,128]{2,1,0:T(8,128)(2,1)} copy(bf16[256,8,128]{0,2,1:T(8,128)(2,1)S(1)} %bitcast.265) | data formatting | bytes 1048576 | tf_op jit(solution)/shard_map/convert_element_type | solution.py:59
  (3 shorter events, 0.0 us)
Async XLA Ops:
  6.5 26.4 %all-gather.2.cloned.1.call-start = ((), (), s32[]{:S(2)}) async-start(), calls=%async_computation | async-start | bytes 1572864 | tf_op jit(solution)/shard_map/all_gather | solution.py:55
  32.9 11.3 %copy-start.1 = (bf16[3,3,3,256,512]{4,3,2,1,0:T(8,128)(2,1)S(1)}, bf16[3,3,3,256,512]{4,3,2,1,0:T(8,128)(2,1)}, u32[]{:S(2)}) copy-start(bf16[3,3,3,256,512]{4,3,2,1,0:T(8,128)(2,1)} %param.4) | copy-start | bytes 21233668
  34.0 7.9 %collective-permute-start = (bf16[512,1,8,16]{0,3,2,1:T(8,128)(2,1)S(1)}, bf16[512,1,8,16]{0,3,2,1:T(8,128)(2,1)S(1)}, u32[]{:S(2)}, u32[]{:S(2)}) collective-permute-start(bf16[512,1,8,16]{0,3,2,1:T(8,128)(2,1)S(1)} %get-tuple-element.20), channel_id=1, source_target_pairs={{0,8},{8,16},{16,24},{1,9},{9,17},{17,25},{2,10},{10,18},{18,26},{... | collective-permute-start | bytes 393224 | tf_op jit(solution)/shard_map/ppermute | solution.py:17
  36.1 5.9 %collective-permute-start.1 = (bf16[512,1,8,16]{0,3,2,1:T(8,128)(2,1)S(1)}, bf16[512,1,8,16]{0,3,2,1:T(8,128)(2,1)S(1)}, u32[]{:S(2)}, u32[]{:S(2)}) collective-permute-start(bf16[512,1,8,16]{0,3,2,1:T(8,128)(2,1)S(1)} %get-tuple-element.19), channel_id=1, source_target_pairs={{8,0},{16,8},{24,16},{9,1},{17,9},{25,17},{10,2},{18,10},{26,18},{... | collective-permute-start | bytes 393224 | tf_op jit(solution)/shard_map/ppermute | solution.py:19
  46.6 6.5 %collective-permute-start.2 = (bf16[512,10,1,16]{0,3,2,1:T(8,128)(2,1)S(1)}, bf16[512,10,1,16]{0,3,2,1:T(8,128)(2,1)S(1)}, u32[]{:S(2)}, u32[]{:S(2)}) collective-permute-start(bf16[512,10,1,16]{0,3,2,1:T(8,128)(2,1)S(1)} %get-tuple-element.14), channel_id=1, source_target_pairs={{0,2},{2,4},{4,6},{1,3},{3,5},{5,7},{8,10},{10,12},{12,14},{9,11},... | collective-permute-start | bytes 491528 | tf_op jit(solution)/shard_map/ppermute | solution.py:17
  50.0 7.8 %collective-permute-start.3 = (bf16[512,10,1,16]{0,3,2,1:T(8,128)(2,1)S(1)}, bf16[512,10,1,16]{0,3,2,1:T(8,128)(2,1)S(1)}, u32[]{:S(2)}, u32[]{:S(2)}) collective-permute-start(bf16[512,10,1,16]{0,3,2,1:T(8,128)(2,1)S(1)} %get-tuple-element.15), channel_id=1, source_target_pairs={{2,0},{4,2},{6,4},{3,1},{5,3},{7,5},{10,8},{12,10},{14,12},{11,9},... | collective-permute-start | bytes 491528 | tf_op jit(solution)/shard_map/ppermute | solution.py:19
  66.3 2.3 %copy-start = (bf16[512,8,8,16]{0,3,2,1:T(8,128)(2,1)S(1)}, bf16[512,8,8,16]{0,3,2,1:T(8,128)(2,1)}, u32[]{:S(2)}) copy-start(bf16[512,8,8,16]{0,3,2,1:T(8,128)(2,1)} %all-gather.2.cloned.1.call-done) | copy-start | bytes 3145732
  68.6 2.6 %copy-start.2 = (f32[256]{0:T(256)S(1)}, f32[256]{0:T(256)}, u32[]{:S(2)}) copy-start(f32[256]{0:T(256)} %param.5) | copy-start | bytes 3076
Sparse Core Ops, SparseCore 0:
  8.9 23.9 all-gather.1
where the time goes:
time: 82.9 us; the launch traced here: 82 us
  waiting for transfers between devices  29.9 us (36%)
  matrix products  18.2 us (22%)
  between operations  13.7 us (17%)
  starting transfers between devices  8.18 us (10%)
  local copies, waits for them, and re-layouts  6.39 us (8%)
  other arithmetic  5.66 us (7%)
    all_gather x1, waiting for transfers between devices, per_device(): gathered = lax.all_gather(blocked, 'ch', axis=0, tiled=True)  24.2 us
    dot_general x27, matrix products, add_taps(): product = jnp.dot(tap_matrix, window, preferred_element_type=jnp.float32)  18.2 us
    ppermute x2, starting transfers between devices, padded(): lax.ppermute(tail, axis, [(i, (i + 1) % count) for i in range(ends)])  5.41 us
    ppermute x2, waiting for transfers between devices, padded(): lax.ppermute(head, axis, [((i + 1) % count, i) for i in range(ends)])  4.72 us
    convert_element_type x1, other arithmetic, per_device(): return result.astype(jnp.bfloat16)  2.85 us
    concatenate x2, other arithmetic, padded(): jnp.concatenate([lax.ppermute(tail, axis, [(i, (i + 1) % count) for i in...  2.81 us
    ppermute x2, starting transfers between devices, padded(): lax.ppermute(head, axis, [((i + 1) % count, i) for i in range(ends)])  2.76 us
    unnamed x8, local copies, waits for them, and re-layouts  2.13 us
  transfers between devices with their start and end apart: 5, of which 3 were waited for; matrix products, arithmetic and copies ran while one was open for 6% of the time, Pallas kernels for 0%

commit v1 on v0

v1 whole, which is shorter than its diff:
```python
import functools

import jax
import jax.numpy as jnp
from jax import lax
from jax.experimental import pallas as pl
from jax.experimental.pallas import tpu as pltpu
from jax.sharding import PartitionSpec as P

CZ = 16
LANES = 128
VMEM = pl.BlockSpec(memory_space=pltpu.VMEM)
bf16, f32 = jnp.bfloat16, jnp.float32


def call(kernel, outs, args, scratch=(), flops=0, limit=24):
    outs = [jax.ShapeDtypeStruct(s, d) for s, d in outs]
    moved = sum(a.size * a.dtype.itemsize for a in [*outs, *args])
    return pl.pallas_call(
        kernel,
        out_shape=outs,
        in_specs=[VMEM] * len(args),
        out_specs=[VMEM] * len(outs),
        scratch_shapes=list(scratch),
        compiler_params=pltpu.CompilerParams(vmem_limit_bytes=limit * 2**20),
        cost_estimate=pl.CostEstimate(flops=flops, bytes_accessed=moved, transcendentals=0),
    )(*args)


def pairs(count, phase):
    found = []
    for low in range(phase, count - 1, 2):
        found += [(low, low + 1), (low + 1, low)]
    return found


def odd(axis):
    return lax.rem(lax.axis_index(axis), 2) == 1


def to_rows(v_ref, rows_ref, first_ref, second_ref, wide):
    cells_x = v_ref.shape[1]
    wide[...] = v_ref[...].astype(f32)
    for x in range(cells_x):
        rows_ref[x] = wide[:, x, :].astype(bf16)
    last = cells_x - 1

    @pl.when(odd("sx"))
    def _():
        first_ref[...] = rows_ref[0]
        second_ref[...] = rows_ref[last]

    @pl.when(jnp.logical_not(odd("sx")))
    def _():
        first_ref[...] = rows_ref[last]
        second_ref[...] = rows_ref[0]


def extended(rows, first, second):
    is_odd = odd("sx")
    before = jnp.where(is_odd, first, second)
    after = jnp.where(is_odd, second, first)
    return [before, *rows, after]


def pack(rows, start):
    cut = [r[:, start : start + CZ] for r in rows]
    part = rows[0].shape[0] // 4
    outer = jnp.concatenate([cut[0], cut[-1]], axis=1)
    folded = jnp.concatenate([outer[g * part : (g + 1) * part] for g in range(4)], axis=1)
    return jnp.concatenate([jnp.concatenate(cut[1:-1], axis=1), folded], axis=0)


def to_strips(rows_ref, first_ref, second_ref, left_ref, right_ref):
    cells_x = rows_ref.shape[0]
    rows = extended([rows_ref[x] for x in range(cells_x)], first_ref[...], second_ref[...])
    low = pack(rows, 0)
    high = pack(rows, LANES - CZ)
    is_odd = odd("sy")
    left_ref[...] = jnp.where(is_odd, low, high)
    right_ref[...] = jnp.where(is_odd, high, low)


def shifted(rows_ref, first_ref, second_ref, strips_ref, xs):
    cells_x, channels, lanes = rows_ref.shape
    part = channels // 4
    size = channels + part
    is_odd = odd("sy")
    one, two = strips_ref[0:size].astype(f32), strips_ref[size : 2 * size].astype(f32)
    before = jnp.where(is_odd, one, two)
    after = jnp.where(is_odd, two, one)
    lane = lax.broadcasted_iota(jnp.int32, (channels, lanes), 1)
    rows = extended([rows_ref[x] for x in range(cells_x)], first_ref[...], second_ref[...])

    def piece(strip, x, to):
        if 1 <= x <= cells_x:
            return pltpu.roll(strip[:channels], (to - (x - 1) * CZ) % lanes, axis=1)
        at = 0 if x == 0 else CZ
        folded = strip[channels:]
        return jnp.concatenate(
            [pltpu.roll(folded, (to - at - g * 2 * CZ) % lanes, axis=1) for g in range(4)], axis=0
        )

    for x in range(cells_x + 2):
        xs[1, x] = rows[x]
        row = rows[x].astype(f32)
        down = pltpu.roll(row, CZ, axis=1)
        xs[0, x] = jnp.where(lane < CZ, piece(before, x, 0), down).astype(bf16)
        up = pltpu.roll(row, lanes - CZ, axis=1)
        xs[2, x] = jnp.where(lane >= lanes - CZ, piece(after, x, lanes - CZ), up).astype(bf16)


def block_sum(weight_ref, xs, at, tile):
    outputs, channels = weight_ref.shape[3], xs.shape[2]
    total = None
    for a in range(3):
        for b in range(3):
            if weight_ref.shape[4] == channels:
                taps = weight_ref[a, b]
            else:
                start = pl.multiple_of(at * channels, channels)
                taps = weight_ref[a, b, :, :, pl.ds(start, channels)]
            window = jnp.concatenate([xs[b, x + a] for x in tile], axis=1)
            product = jnp.dot(
                taps.reshape(3 * outputs, channels), window, preferred_element_type=f32
            )
            total = product if total is None else total + product
    return total


def tiles_of(cells_x):
    inner = [(x, x + 1) for x in range(1, cells_x - 1, 2)]
    return [*inner, (0, cells_x - 1)]


def own_kernel(rows_ref, first_ref, second_ref, strips_ref, weight_ref, acc_ref, xs):
    at = lax.axis_index("ch")
    shifted(rows_ref, first_ref, second_ref, strips_ref, xs)
    for tile in tiles_of(rows_ref.shape[0]):
        total = block_sum(weight_ref, xs, at, tile)
        for j, x in enumerate(tile):
            acc_ref[x] = total[:, j * LANES : (j + 1) * LANES]


def other_kernel(step, final, *refs):
    rows_ref, first_ref, second_ref, strips_ref, weight_ref, acc_ref = refs[:6]
    count = lax.axis_size("ch")
    at = lax.rem(lax.axis_index("ch") + count - step, count)
    xs = refs[-2]
    shifted(rows_ref, first_ref, second_ref, strips_ref, xs)
    if final:
        bias_ref, out_ref, wide = refs[6], refs[7], refs[-1]
        outputs = bias_ref.shape[0]
        cell = lax.rem(lax.broadcasted_iota(jnp.int32, (outputs, LANES), 1), CZ)
    else:
        sum_ref = refs[6]
    for tile in tiles_of(rows_ref.shape[0]):
        total = block_sum(weight_ref, xs, at, tile)
        for j, x in enumerate(tile):
            row = acc_ref[x] + total[:, j * LANES : (j + 1) * LANES]
            if not final:
                sum_ref[x] = row
                continue
            under, mid, over = (row[c * outputs : (c + 1) * outputs] for c in range(3))
            under = jnp.where(cell == 0, 0.0, pltpu.roll(under, 1, axis=1))
            over = jnp.where(cell == CZ - 1, 0.0, pltpu.roll(over, LANES - 1, axis=1))
            wide[:, x, :] = (under + over) + mid + bias_ref[...]
    if final:
        out_ref[...] = wide[...].astype(bf16)


def per_device(volume, weight, bias):
    channels, cells_x, lanes = volume.shape
    outputs = weight.shape[3]
    count, count_x, count_y = (lax.axis_size(a) for a in ("ch", "sx", "sy"))
    strip = channels + channels // 4
    face, taps = (channels, lanes), (3 * outputs, lanes)
    flops = 2 * 27 * channels * outputs * cells_x * lanes

    def along(step):
        return [(i, (i + step) % count) for i in range(count)]

    def rows_of(block):
        return call(
            to_rows,
            [((cells_x, *face), bf16), (face, bf16), (face, bf16)],
            [block],
            [pltpu.VMEM((channels, cells_x, lanes), f32)],
        )

    others = [lax.ppermute(volume, "ch", along(step)) for step in range(1, count)]
    spread = jnp.broadcast_to(bias[:, None], (outputs, lanes))
    rows, one, two = rows_of(volume)
    first = lax.ppermute(one, "sx", pairs(count_x, 0))
    second = lax.ppermute(two, "sx", pairs(count_x, 1))
    left, right = call(to_strips, [((strip, lanes), bf16)] * 2, [rows, first, second])
    strips = jnp.concatenate(
        [lax.ppermute(left, "sy", pairs(count_y, 0)), lax.ppermute(right, "sy", pairs(count_y, 1))]
    )
    other_strips = [lax.ppermute(strips, "ch", along(step)) for step in range(1, count)]
    other_seconds = [
        lax.ppermute(
            second,
            ("sx", "ch"),
            [(x * count + i, x * count + j) for x in range(1, count_x - 1) for i, j in along(step)],
        )
        for step in range(1, count)
    ]
    def weight_of(step):
        if channels % LANES == 0:
            return weight
        at = lax.rem(lax.axis_index("ch") + count - step, count)
        return lax.dynamic_slice_in_dim(weight, at * channels, channels, axis=4)

    xs = pltpu.VMEM((3, cells_x + 2, *face), bf16)
    (acc,) = call(
        own_kernel,
        [((cells_x, *taps), f32)],
        [rows, first, second, strips, weight_of(0)],
        [xs],
        flops,
    )
    for step in range(1, count):
        block, block_one, _ = rows_of(others[step - 1])
        block_first = lax.ppermute(block_one, "sx", pairs(count_x, 0))
        args = [block, block_first, other_seconds[step - 1], other_strips[step - 1]]
        args += [weight_of(step), acc]
        final = step == count - 1
        if final:
            args.append(spread)
        (acc,) = call(
            functools.partial(other_kernel, step, final),
            [((outputs, cells_x, lanes), bf16) if final else ((cells_x, *taps), f32)],
            args,
            [xs, pltpu.VMEM((outputs, cells_x, lanes), f32)],
            flops,
        )
    return acc


def solution(mesh):
    return jax.shard_map(
        per_device,
        mesh=mesh,
        in_specs=(P("ch", "sx", "sy"), P(None, None, None, "ch", None), P("ch")),
        out_specs=P("ch", "sx", "sy"),
        check_vma=False,
    )
```

time: 82.9 us -> 35.1 us (0.42)
  the two profiles are of different devices: /device:TPU:0 before, /device:TPU:11 now
where the time goes in v1:
time: 35.1 us; the launch traced here: 34.8 us
  starting transfers between devices  14.6 us (42%)
  Pallas kernels  13.6 us (39%)
  local copies, waits for them, and re-layouts  4.2 us (12%)
  waiting for transfers between devices  2.31 us (7%)
    pallas_call x5, Pallas kernels, call(): pl.pallas_call(kernel, out_shape=outs, in_specs=[VMEM] * len(args), out_s...  13.6 us
    ppermute x1, starting transfers between devices, per_device(): block_first = lax.ppermute(block_one, 'sx', pairs(count_x, 0))  4.91 us
    ppermute x1, starting transfers between devices, per_device(): lax.ppermute(right, 'sy', pairs(count_y, 1))  4.32 us
    unnamed x9, local copies, waits for them, and re-layouts  4.1 us
    ppermute x1, starting transfers between devices, per_device(): first = lax.ppermute(one, 'sx', pairs(count_x, 0))  2.27 us
    ppermute x1, waiting for transfers between devices, per_device(): lax.ppermute(right, 'sy', pairs(count_y, 1))  1.4 us
    ppermute x1, starting transfers between devices, per_device(): lax.ppermute(volume, 'ch', along(step))  1.24 us
    ppermute x1, waiting for transfers between devices, per_device(): first = lax.ppermute(one, 'sx', pairs(count_x, 0))  0.9 us
  transfers between devices with their start and end apart: 8, of which 2 were waited for; matrix products, arithmetic and copies ran while one was open for 0% of the time, Pallas kernels for 23%

profile of v1, /device:TPU:11, one launch (start us, length us, event | category | flops | bytes accessed | tf_op | source)
XLA Modules:
  0.0 34.8 jit_solution(1679128974076077934)
XLA Ops:
  0.0 1.2 %collective-permute-start = (bf16[256,8,128]{2,1,0:T(8,128)(2,1)}, bf16[256,8,128]{2,1,0:T(8,128)(2,1)S(1)}, u32[]{:S(2)}, u32[]{:S(2)}) collective-permute-start(bf16[256,8,128]{2,1,0:T(8,128)(2,1)} %v_ref.1), channel_id=1, source_target_pairs={{0,1},{1,0},{2,3},{3,2},{4,5},{5,4},{6,7},{7,6},{8,9},{9,8},{10,11... | collective-permute-start | bytes 1572872 | tf_op jit(solution)/shard_map/ppermute | solution.py:191
  1.2 0.0 copy-start
  1.2 1.1 %copy-done = bf16[256,8,128]{2,1,0:T(8,128)(2,1)S(1)} copy-done((bf16[256,8,128]{2,1,0:T(8,128)(2,1)S(1)}, bf16[256,8,128]{2,1,0:T(8,128)(2,1)}, u32[]{:S(2)}) %copy-start) | copy-done | bytes 524312
  2.3 1.5 %shard_map.38 = (bf16[8,256,128]{2,1,0:T(8,128)(2,1)S(1)}, bf16[256,128]{1,0:T(8,128)(2,1)S(1)}, bf16[256,128]{1,0:T(8,128)(2,1)S(1)}) custom-call(bf16[256,8,128]{2,1,0:T(8,128)(2,1)S(1)} %copy-done), custom_call_target="tpu_custom_call" | custom-call | bytes 1179648 | tf_op jit(solution)/shard_map/pallas_call | solution.py:19
  3.8 0.7 %collective-permute-start.2 = (bf16[256,128]{1,0:T(8,128)(2,1)S(1)}, bf16[256,128]{1,0:T(8,128)(2,1)S(1)}, u32[]{:S(2)}, u32[]{:S(2)}) collective-permute-start(bf16[256,128]{1,0:T(8,128)(2,1)S(1)} %get-tuple-element.14), channel_id=1, source_target_pairs={{8,16},{16,8},{9,17},{17,9},{10,18},{18,10},{11,19},{19,11},{12,20... | collective-permute-start | bytes 196616 | tf_op jit(solution)/shard_map/ppermute | solution.py:195
  4.5 2.3 %collective-permute-start.4 = (bf16[256,128]{1,0:T(8,128)(2,1)S(1)}, bf16[256,128]{1,0:T(8,128)(2,1)S(1)}, u32[]{:S(2)}, u32[]{:S(2)}) collective-permute-start(bf16[256,128]{1,0:T(8,128)(2,1)S(1)} %get-tuple-element.16), channel_id=1, source_target_pairs={{0,8},{8,0},{16,24},{24,16},{1,9},{9,1},{17,25},{25,17},{2,10},{10... | collective-permute-start | bytes 196616 | tf_op jit(solution)/shard_map/ppermute | solution.py:194
  6.7 0.0 collective-permute-done.2.second_ref
  6.7 0.9 %collective-permute-done.4.first_ref = bf16[256,128]{1,0:T(8,128)(2,1)S(1)} collective-permute-done((bf16[256,128]{1,0:T(8,128)(2,1)S(1)}, bf16[256,128]{1,0:T(8,128)(2,1)S(1)}, u32[]{:S(2)}, u32[]{:S(2)}) %collective-permute-start.4) | collective-permute-done | bytes 65568 | tf_op jit(solution)/shard_map/ppermute | solution.py:194
  7.6 0.5 %shard_map.39 = (bf16[320,128]{1,0:T(8,128)(2,1)S(1)}, bf16[320,128]{1,0:T(8,128)(2,1)S(1)}) custom-call(bf16[8,256,128]{2,1,0:T(8,128)(2,1)S(1)} %get-tuple-element.15.rows_ref, bf16[256,128]{1,0:T(8,128)(2,1)S(1)} %collective-permute-done.4.first_ref, bf16[256,128]{1,0:T(8,128)(2,1)S(1)} %collective-permute-done.2.second_ref), custom_call_target="tpu_custom_call" | custom-call | bytes 819200 | tf_op jit(solution)/shard_map/pallas_call | solution.py:19
  8.1 0.2 collective-permute-start.5
  8.3 4.3 %collective-permute-start.6 = (bf16[320,128]{1,0:T(8,128)(2,1)S(1)}, bf16[320,128]{1,0:T(8,128)(2,1)S(1)}, u32[]{:S(2)}, u32[]{:S(2)}) collective-permute-start(bf16[320,128]{1,0:T(8,128)(2,1)S(1)} %get-tuple-element.18), channel_id=1, source_target_pairs={{2,4},{4,2},{3,5},{5,3},{10,12},{12,10},{11,13},{13,11},{18,20},{2... | collective-permute-start | bytes 245768 | tf_op jit(solution)/shard_map/ppermute | solution.py:198
  12.7 0.7 %collective-permute-start.3 = (bf16[256,128]{1,0:T(8,128)(2,1)S(1)}, bf16[256,128]{1,0:T(8,128)(2,1)S(1)}, u32[]{:S(2)}, u32[]{:S(2)}) collective-permute-start(bf16[256,128]{1,0:T(8,128)(2,1)S(1)} %collective-permute-done.2.second_ref), channel_id=1, source_target_pairs={{8,9},{9,8},{16,17},{17,16},{10,11},{11,10},{18,19},{19,18},{12,13... | collective-permute-start | bytes 196616 | tf_op jit(solution)/shard_map/ppermute | solution.py:202
  13.3 0.0 collective-permute-done.5
  13.3 0.0 copy-start.3
  13.4 1.4 %collective-permute-done.6 = bf16[320,128]{1,0:T(8,128)(2,1)S(1)} collective-permute-done((bf16[320,128]{1,0:T(8,128)(2,1)S(1)}, bf16[320,128]{1,0:T(8,128)(2,1)S(1)}, u32[]{:S(2)}, u32[]{:S(2)}) %collective-permute-start.6) | collective-permute-done | bytes 81952 | tf_op jit(solution)/shard_map/ppermute | solution.py:198
  14.8 0.3 collective-permute-start.7
  15.1 0.0 collective-permute-done.v_ref
  15.1 2.1 %shard_map.37 = (bf16[8,256,128]{2,1,0:T(8,128)(2,1)S(1)}, bf16[256,128]{1,0:T(8,128)(2,1)S(1)}, bf16[256,128]{1,0:T(8,128)(2,1)}) custom-call(bf16[256,8,128]{2,1,0:T(8,128)(2,1)S(1)} %collective-permute-done.v_ref), custom_call_target="tpu_custom_call" | custom-call | bytes 1179648 | tf_op jit(solution)/shard_map/pallas_call | solution.py:19
  17.2 4.9 %collective-permute-start.1 = (bf16[256,128]{1,0:T(8,128)(2,1)S(1)}, bf16[256,128]{1,0:T(8,128)(2,1)S(1)}, u32[]{:S(2)}, u32[]{:S(2)}) collective-permute-start(bf16[256,128]{1,0:T(8,128)(2,1)S(1)} %get-tuple-element.13), channel_id=1, source_target_pairs={{0,8},{8,0},{16,24},{24,16},{1,9},{9,1},{17,25},{25,17},{2,10},{10... | collective-permute-start | bytes 196616 | tf_op jit(solution)/shard_map/ppermute | solution.py:225
  22.1 0.0 copy-start.1
  22.1 3.0 %copy-done.1 = bf16[3,3,3,256,512]{4,3,2,1,0:T(8,128)(2,1)S(1)} copy-done((bf16[3,3,3,256,512]{4,3,2,1,0:T(8,128)(2,1)S(1)}, bf16[3,3,3,256,512]{4,3,2,1,0:T(8,128)(2,1)}, u32[]{:S(2)}) %copy-start.1) | copy-done | bytes 7077912
  25.1 0.0 copy-start.2
  25.1 4.0 %shard_map.40.refs_5_ = f32[8,768,128]{2,1,0:T(8,128)S(1)} custom-call(bf16[8,256,128]{2,1,0:T(8,128)(2,1)S(1)} %get-tuple-element.15.rows_ref, bf16[256,128]{1,0:T(8,128)(2,1)S(1)} %collective-permute-done.4.first_ref, bf16[256,128]{1,0:T(8,128)(2,1)S(1)} %collective-permute-done.2.second_ref, ...), custom_call_target="tpu_custom_call" | custom-call | flops 3623878656 | bytes 11042816 | tf_op jit(solution)/shard_map/pallas_call | solution.py:19
  29.1 0.0 collective-permute-done.3.refs_2_
  29.1 0.0 collective-permute-done.7.refs_3_
  29.1 0.0 collective-permute-done.1.refs_1_
  29.1 0.0 copy-done.3
  29.1 0.1 broadcast_in_dim.2.refs_6_
  29.2 0.0 copy-done.2
  29.3 5.6 %shard_map.41 = bf16[256,8,128]{2,1,0:T(8,128)(2,1)} custom-call(bf16[8,256,128]{2,1,0:T(8,128)(2,1)S(1)} %get-tuple-element.12.refs_0_, bf16[256,128]{1,0:T(8,128)(2,1)S(1)} %collective-permute-done.1.refs_1_, bf16[256,128]{1,0:T(8,128)(2,1)S(1)} %collective-permute-done.3.refs_2_, bf16[640,128]{1,0:T(8,128)(2,1)S(1)} %collective-permute-done.7.refs_3_, ...), custom_call_target="tpu_custom_call" | custom-call | flops 3623878656 | bytes 11698176 | tf_op jit(solution)/shard_map/pallas_call | solution.py:19
  (2 shorter events, 0.0 us)
Async XLA Ops:
  0.0 15.1 %collective-permute-start = (bf16[256,8,128]{2,1,0:T(8,128)(2,1)}, bf16[256,8,128]{2,1,0:T(8,128)(2,1)S(1)}, u32[]{:S(2)}, u32[]{:S(2)}) collective-permute-start(bf16[256,8,128]{2,1,0:T(8,128)(2,1)} %v_ref.1), channel_id=1, source_target_pairs={{0,1},{1,0},{2,3},{3,2},{4,5},{5,4},{6,7},{7,6},{8,9},{9,8},{10,11... | collective-permute-start | bytes 1572872 | tf_op jit(solution)/shard_map/ppermute | solution.py:191
  1.2 1.1 %copy-start = (bf16[256,8,128]{2,1,0:T(8,128)(2,1)S(1)}, bf16[256,8,128]{2,1,0:T(8,128)(2,1)}, u32[]{:S(2)}) copy-start(bf16[256,8,128]{2,1,0:T(8,128)(2,1)} %v_ref.1) | copy-start | bytes 1572868
  3.8 2.9 %collective-permute-start.2 = (bf16[256,128]{1,0:T(8,128)(2,1)S(1)}, bf16[256,128]{1,0:T(8,128)(2,1)S(1)}, u32[]{:S(2)}, u32[]{:S(2)}) collective-permute-start(bf16[256,128]{1,0:T(8,128)(2,1)S(1)} %get-tuple-element.14), channel_id=1, source_target_pairs={{8,16},{16,8},{9,17},{17,9},{10,18},{18,10},{11,19},{19,11},{12,20... | collective-permute-start | bytes 196616 | tf_op jit(solution)/shard_map/ppermute | solution.py:195
  4.5 3.2 %collective-permute-start.4 = (bf16[256,128]{1,0:T(8,128)(2,1)S(1)}, bf16[256,128]{1,0:T(8,128)(2,1)S(1)}, u32[]{:S(2)}, u32[]{:S(2)}) collective-permute-start(bf16[256,128]{1,0:T(8,128)(2,1)S(1)} %get-tuple-element.16), channel_id=1, source_target_pairs={{0,8},{8,0},{16,24},{24,16},{1,9},{9,1},{17,25},{25,17},{2,10},{10... | collective-permute-start | bytes 196616 | tf_op jit(solution)/shard_map/ppermute | solution.py:194
  8.1 5.2 %collective-permute-start.5 = (bf16[320,128]{1,0:T(8,128)(2,1)S(1)}, bf16[320,128]{1,0:T(8,128)(2,1)S(1)}, u32[]{:S(2)}, u32[]{:S(2)}) collective-permute-start(bf16[320,128]{1,0:T(8,128)(2,1)S(1)} %get-tuple-element.17), channel_id=1, source_target_pairs={{0,2},{2,0},{4,6},{6,4},{1,3},{3,1},{5,7},{7,5},{8,10},{10,8},{12,... | collective-permute-start | bytes 245768 | tf_op jit(solution)/shard_map/ppermute | solution.py:198
  8.3 6.4 %collective-permute-start.6 = (bf16[320,128]{1,0:T(8,128)(2,1)S(1)}, bf16[320,128]{1,0:T(8,128)(2,1)S(1)}, u32[]{:S(2)}, u32[]{:S(2)}) collective-permute-start(bf16[320,128]{1,0:T(8,128)(2,1)S(1)} %get-tuple-element.18), channel_id=1, source_target_pairs={{2,4},{4,2},{3,5},{5,3},{10,12},{12,10},{11,13},{13,11},{18,20},{2... | collective-permute-start | bytes 245768 | tf_op jit(solution)/shard_map/ppermute | solution.py:198
  12.7 16.5 %collective-permute-start.3 = (bf16[256,128]{1,0:T(8,128)(2,1)S(1)}, bf16[256,128]{1,0:T(8,128)(2,1)S(1)}, u32[]{:S(2)}, u32[]{:S(2)}) collective-permute-start(bf16[256,128]{1,0:T(8,128)(2,1)S(1)} %collective-permute-done.2.second_ref), channel_id=1, source_target_pairs={{8,9},{9,8},{16,17},{17,16},{10,11},{11,10},{18,19},{19,18},{12,13... | collective-permute-start | bytes 196616 | tf_op jit(solution)/shard_map/ppermute | solution.py:202
  13.3 15.8 %copy-start.3 = (f32[256]{0:T(256)S(1)}, f32[256]{0:T(256)}, u32[]{:S(2)}) copy-start(f32[256]{0:T(256)} %param.5) | copy-start | bytes 3076
  14.8 14.3 %collective-permute-start.7 = (bf16[640,128]{1,0:T(8,128)(2,1)S(1)}, bf16[640,128]{1,0:T(8,128)(2,1)S(1)}, u32[]{:S(2)}, u32[]{:S(2)}) collective-permute-start(bf16[640,128]{1,0:T(8,128)(2,1)S(1)} %constant_dynamic-update-slice_fusion.strips_ref), channel_id=1, source_target_pairs={{0,1},{1,0},{2,3},{3,2},{4,5},{5,4},{6,7},{7,6},{8,9},{9,8},{10,11... | collective-permute-start | bytes 491528 | tf_op jit(solution)/shard_map/ppermute | solution.py:200
  17.2 12.0 %collective-permute-start.1 = (bf16[256,128]{1,0:T(8,128)(2,1)S(1)}, bf16[256,128]{1,0:T(8,128)(2,1)S(1)}, u32[]{:S(2)}, u32[]{:S(2)}) collective-permute-start(bf16[256,128]{1,0:T(8,128)(2,1)S(1)} %get-tuple-element.13), channel_id=1, source_target_pairs={{0,8},{8,0},{16,24},{24,16},{1,9},{9,1},{17,25},{25,17},{2,10},{10... | collective-permute-start | bytes 196616 | tf_op jit(solution)/shard_map/ppermute | solution.py:225
  22.1 3.0 %copy-start.1 = (bf16[3,3,3,256,512]{4,3,2,1,0:T(8,128)(2,1)S(1)}, bf16[3,3,3,256,512]{4,3,2,1,0:T(8,128)(2,1)}, u32[]{:S(2)}) copy-start(bf16[3,3,3,256,512]{4,3,2,1,0:T(8,128)(2,1)} %refs_4_.1) | copy-start | bytes 21233668
  25.1 4.2 %copy-start.2 = (bf16[3,3,3,256,512]{4,3,2,1,0:T(8,128)(2,1)S(1)}, bf16[3,3,3,256,512]{4,3,2,1,0:T(8,128)(2,1)}, u32[]{:S(2)}) copy-start(bf16[3,3,3,256,512]{4,3,2,1,0:T(8,128)(2,1)} %refs_4_.1) | copy-start | bytes 21233668
